TPU v7x, 256 devices: a whole 4x4x8 slice. The times are simulated.
256 devices in a mesh: rows: 32 (over z, x), rhs: 8 (over y, core).
Axes of the slice: x: 4, y: 4, z: 8, core: 2. Of those that a mesh axis runs over, the one named last changes fastest.
Arguments:
- right_side: float32 [32768, 1024], P('rows', 'rhs'), may hold values from -6 to 6
- leaf_blocks: bfloat16 [128, 2, 256, 256], P('rows'), may hold values from -0.25 to 0.25
- out_basis: bfloat16 [128, 2, 256, 128], P('rows'), may hold values from -0.375 to 0.375
- in_basis: bfloat16 [128, 2, 256, 128], P('rows'), may hold values from -0.25 to 0.25
- couplings: bfloat16 [128, 7, 2, 128, 128], P('rows'), may hold values from -6 to 6
Outputs:
- solution: float32 [2, 32768, 1024], P(None, 'rows', 'rhs')
All inputs are finite; a program needn't handle non-finite values.
Results may differ from a plain program's by a relative error of at most 0.0043.
Values sent between devices are 32-bit elements; how exact they have to be, the bound alone decides.
No kernel may reach another device: no remote copies, remote signals or barrier semaphores. Data moves between devices by JAX's collectives and lax.ppermute only.
A program may use at most 64 MiB of HBM per device.

v0:
```python
import math
import jax
import jax.numpy as jnp
from jax import lax
from jax.sharding import PartitionSpec as P


def dft_table(length, phase_sign):
    indices = jnp.arange(length, dtype=jnp.int32)
    product = indices[:, None] * indices[None, :] % length
    angles = 2.0 * math.pi / length * product.astype(jnp.float32)
    return (jnp.cos(angles), phase_sign * jnp.sin(angles))


def exact_mix(pattern, left_re, left_im, right_re, right_im):
    highest = lax.Precision.HIGHEST
    real_part = jnp.einsum(pattern, left_re, right_re, precision=highest) - jnp.einsum(
        pattern, left_im, right_im, precision=highest
    )
    imag_part = jnp.einsum(pattern, left_re, right_im, precision=highest) + jnp.einsum(
        pattern, left_im, right_re, precision=highest
    )
    return (real_part, imag_part)


def narrow_mix(pattern, left_re, left_im, right_re, right_im):
    real_part = jnp.einsum(
        pattern, left_re, right_re, preferred_element_type=jnp.float32
    ) - jnp.einsum(pattern, left_im, right_im, preferred_element_type=jnp.float32)
    imag_part = jnp.einsum(
        pattern, left_re, right_im, preferred_element_type=jnp.float32
    ) + jnp.einsum(pattern, left_im, right_re, preferred_element_type=jnp.float32)
    return (real_part, imag_part)


def local_dft(values_re, values_im, phase_sign):
    length, columns = values_re.shape
    first = 2 ** ((length.bit_length() - 1) // 2)
    second = length // first
    table_re, table_im = dft_table(first, phase_sign)
    grid_re = values_re.reshape(first, second, columns)
    highest = lax.Precision.HIGHEST
    if values_im is None:
        part_re = jnp.einsum("kh,hlc->klc", table_re, grid_re, precision=highest)
        part_im = jnp.einsum("kh,hlc->klc", table_im, grid_re, precision=highest)
    else:
        grid_im = values_im.reshape(first, second, columns)
        part_re, part_im = exact_mix("kh,hlc->klc", table_re, table_im, grid_re, grid_im)
    low_index = jnp.arange(first, dtype=jnp.int32)
    high_index = jnp.arange(second, dtype=jnp.int32)
    twist = (low_index[:, None] * high_index[None, :] % length).astype(jnp.float32) * (
        2.0 * math.pi / length
    )
    twist_re = jnp.cos(twist)[:, :, None]
    twist_im = phase_sign * jnp.sin(twist)[:, :, None]
    turned_re = part_re * twist_re - part_im * twist_im
    turned_im = part_re * twist_im + part_im * twist_re
    outer_re, outer_im = dft_table(second, phase_sign)
    result_re, result_im = exact_mix("jl,klc->jkc", outer_re, outer_im, turned_re, turned_im)
    return (result_re.reshape(length, columns), result_im.reshape(length, columns))


def sibling_sum(values, group):
    count, rank_size, columns = values.shape
    grouped = values.reshape(count // (2 * group), 2, group, rank_size, columns).sum(axis=2)
    swapped = grouped[:, ::-1]
    spread = jnp.broadcast_to(
        swapped[:, :, None], (count // (2 * group), 2, group, rank_size, columns)
    )
    return spread.reshape(count, rank_size, columns)


def shards(right_side, leaf_blocks, out_basis, in_basis, couplings):
    rows_count = lax.axis_size("rows")
    device = lax.axis_index("rows")
    length, columns = right_side.shape
    full_order = length * rows_count
    band_size = length // rows_count
    norm_factor = 1.0 / math.sqrt(full_order)
    positions = jnp.arange(length, dtype=jnp.int32)
    phases = (device * positions % full_order).astype(jnp.float32) * (2.0 * math.pi / full_order)
    phase_re = jnp.cos(phases)[:, None]
    phase_im = jnp.sin(phases)[:, None]
    local_re, local_im = local_dft(right_side, None, -1.0)
    turned = jnp.stack(
        [local_re * phase_re + local_im * phase_im, local_im * phase_re - local_re * phase_im]
    )
    turned = turned.reshape(2, rows_count, band_size, columns)
    across_re, across_im = dft_table(rows_count, -1.0)
    blocks = lax.all_to_all(turned, "rows", split_axis=1, concat_axis=1, tiled=True)
    mixed_re, mixed_im = exact_mix("jd,dqc->jqc", across_re, across_im, blocks[0], blocks[1])
    ordered = (jnp.stack([mixed_re, mixed_im]) * norm_factor).astype(jnp.bfloat16)
    leaf_count = out_basis.shape[0]
    leaf_size = out_basis.shape[2]
    rank_size = out_basis.shape[3]
    level_count = couplings.shape[1]
    inner_levels = leaf_count.bit_length() - 1
    up_levels = rows_count.bit_length() - 1
    leaves = ordered.reshape(2, leaf_count, leaf_size, columns)
    coeff_re, coeff_im = narrow_mix(
        "lar,lac->lrc", in_basis[:, 0], -in_basis[:, 1], leaves[0], leaves[1]
    )
    inner_re = []
    inner_im = []
    for level_index in range(inner_levels):
        group = 2**level_index
        weight = (2.0 * rank_size * level_count * group) ** (-0.5)
        inner_re.append((weight * sibling_sum(coeff_re, group)).astype(jnp.bfloat16))
        inner_im.append((weight * sibling_sum(coeff_im, group)).astype(jnp.bfloat16))
    field_re, field_im = narrow_mix(
        "ltrs,tlsc->lrc",
        couplings[:, :inner_levels, 0],
        couplings[:, :inner_levels, 1],
        jnp.stack(inner_re),
        jnp.stack(inner_im),
    )
    totals = jnp.stack([jnp.sum(coeff_re, axis=0), jnp.sum(coeff_im, axis=0)])
    every = lax.all_gather(totals[None], "rows", axis=0, tiled=True)
    device_ids = jnp.arange(rows_count, dtype=jnp.int32)
    bit_ids = jnp.arange(up_levels, dtype=jnp.int32)
    partner_group = jnp.bitwise_xor(jnp.right_shift(device, bit_ids), 1)
    member = (
        jnp.right_shift(device_ids[None, :], bit_ids[:, None]) == partner_group[:, None]
    ).astype(jnp.float32)
    groups = jnp.einsum("ud,dkrc->ukrc", member, every, precision=lax.Precision.HIGHEST)
    scales = jnp.asarray(
        [
            (2.0 * rank_size * level_count * 2 ** (inner_levels + bit_index)) ** (-0.5)
            for bit_index in range(up_levels)
        ],
        jnp.float32,
    )
    across = (groups * scales[:, None, None, None]).astype(jnp.bfloat16)
    cross_re, cross_im = narrow_mix(
        "lurs,usc->lrc",
        couplings[:, inner_levels:, 0],
        couplings[:, inner_levels:, 1],
        across[:, 0],
        across[:, 1],
    )
    field_low_re = (field_re + cross_re).astype(jnp.bfloat16)
    field_low_im = (field_im + cross_im).astype(jnp.bfloat16)
    far_re, far_im = narrow_mix(
        "lar,lrc->lac", out_basis[:, 0], out_basis[:, 1], field_low_re, field_low_im
    )
    own_re, own_im = narrow_mix(
        "lab,lbc->lac", leaf_blocks[:, 0], leaf_blocks[:, 1], leaves[0], leaves[1]
    )
    image = jnp.stack([own_re + far_re, own_im + far_im])
    image = image.reshape(2, rows_count, band_size, columns)
    back_re, back_im = dft_table(rows_count, 1.0)
    spectral_re, spectral_im = exact_mix("jd,dqc->jqc", back_re, back_im, image[0], image[1])
    blocks = lax.all_to_all(
        jnp.stack([spectral_re, spectral_im]), "rows", split_axis=1, concat_axis=1, tiled=True
    )
    count = blocks.shape[3]
    flat_re = blocks[0].reshape(length, count)
    flat_im = blocks[1].reshape(length, count)
    rolled_re = flat_re * phase_re - flat_im * phase_im
    rolled_im = flat_re * phase_im + flat_im * phase_re
    result_re, result_im = local_dft(rolled_re, rolled_im, 1.0)
    return jnp.stack([result_re, result_im]) * norm_factor


def solution(mesh):
    placed = (
        P("rows", "rhs"),
        P("rows", None, None, None),
        P("rows", None, None, None),
        P("rows", None, None, None),
        P("rows", None, None, None, None),
    )
    return jax.shard_map(
        shards, mesh=mesh, in_specs=placed, out_specs=P(None, "rows", "rhs"), check_vma=False
    )
```

profile of v0, /device:TPU:2, one launch (start us, length us, event | category | flops | bytes accessed | tf_op | source)
XLA Modules:
  0.0 204.1 jit_solution(9726625276925699508)
XLA Ops:
  7.1 0.5 copy-done
  7.6 0.9 fusion.65
  8.5 1.0 multiply_add_fusion.2
  9.5 0.9 fusion.57
  10.4 0.9 fusion.61
  11.3 0.9 convolution_add_fusion.5
  12.2 1.0 add_bitcast_fusion
  13.3 0.6 copy.94
  14.0 39.5 %all_to_all.10 = f32[2,32,32,128]{3,2,0,1:T(8,128)S(1)} all-to-all(f32[2,32,32,128]{3,2,0,1:T(8,128)S(1)} %copy.94), channel_id=1, replica_groups=mesh['rows'=32,'rhs'=8] {'rows'}, dimensions={1} | all-to-all | bytes 2097152 | tf_op jit(solution)/shard_map/all_to_all | solution.py:90
  53.5 0.9 fusion.43
  54.4 0.9 fusion.44
  55.3 0.9 fusion.15
  56.2 0.9 fusion.14
  57.2 0.1 fusion.28
  57.3 0.1 copy.97
  57.6 0.6 copy-done.3
  58.2 0.3 fusion.84
  58.5 0.3 fusion.82
  58.7 0.3 bitcast_reduce_fusion.1
  59.0 0.3 bitcast_reduce_fusion
  59.3 0.8 copy.111
  60.1 0.6 shift-right-arithmetic_xor_fusion
  61.0 1.0 convolution_bitcast_fusion.2
  62.0 0.9 convolution_bitcast_fusion.6
  62.9 0.3 fusion.39
  63.2 0.3 fusion.41
  63.6 1.1 convolution_add_fusion.6
  64.7 1.1 convolution_subtract_fusion.6
  65.8 71.9 %all-gather.3.cloned.1.call-done = f32[64,128,128]{2,1,0:T(8,128)} async-done(((f32[2,128,128]{2,1,0:T(8,128)}), f32[64,128,128]{2,1,0:T(8,128)}) %all-gather.3.cloned.1.call-update) | async-done | bytes 4194320 | tf_op jit(solution)/shard_map/all_gather | solution.py:118
  137.7 5.8 %fusion.5 = bf16[5,2,128,128]{3,0,2,1:T(8,128)(2,1)S(1)} fusion(f32[32,2,128,128]{3,2,1,0:T(8,128)} %bitcast.317, f32[5]{0:T(128)S(1)} %copy-done.21, s32[5]{0:T(128)S(1)} %copy-done.22), kind=kOutput, calls=%fused_computation.3 | convolution fusion | flops 63242560 | bytes 4522024 | tf_op jit(solution)/shard_map/ud,dkrc->ukrc/dot_general | solution.py:125
  143.6 0.2 copy.116
  143.8 0.2 copy.114
  144.0 0.4 convolution_bitcast_fusion
  144.4 0.3 convolution_bitcast_fusion.4
  144.8 0.3 fusion.25
  145.2 0.3 fusion.23
  145.6 0.2 fusion.26
  145.9 0.2 fusion.27
  146.1 0.2 copy-done.4
  146.3 0.2 fusion.75
  146.5 0.2 fusion.73
  146.8 0.2 fusion.11
  147.0 0.2 copy.125
  147.2 0.4 copy-done.5
  147.6 0.4 fusion.13
  148.0 0.2 copy.121
  148.2 0.9 fusion.55
  149.1 0.9 fusion.51
  150.1 0.9 fusion.9
  151.0 0.9 fusion.8
  151.9 1.6 copy.129
  153.5 7.6 %all-to-all-start.1 = ((f32[2,32,32,128]{3,2,0,1:T(8,128)}), f32[2,32,32,128]{3,2,0,1:T(8,128)S(1)}, u32[]{:S(2)}, u32[]{:S(2)}) async-start(f32[2,32,32,128]{3,2,0,1:T(8,128)} %copy.129), calls=%async_computation.1 | async-start | bytes 2097152 | tf_op jit(solution)/shard_map/all_to_all | solution.py:153
  161.3 25.3 %all-to-all-done.1 = f32[2,32,32,128]{3,2,0,1:T(8,128)S(1)} async-done(((f32[2,32,32,128]{3,2,0,1:T(8,128)}), f32[2,32,32,128]{3,2,0,1:T(8,128)S(1)}, u32[]{:S(2)}, u32[]{:S(2)}) %all-to-all-start.1) | async-done | bytes 1048608 | tf_op jit(solution)/shard_map/all_to_all | solution.py:153
  186.6 1.3 fusion.103
  187.9 1.3 fusion.102
  189.2 1.3 convolution_subtract_fusion.1
  190.6 1.4 multiply_subtract_fusion
  192.0 0.9 fusion.49
  192.9 0.9 fusion.45
  193.8 0.9 convolution_subtract_fusion
  194.7 0.9 convolution_add_fusion
  195.6 0.3 copy.138
  195.9 0.3 copy.135
  196.2 1.1 maximum_multiply_fusion.1
  (69 shorter events, 1.5 us)
Async XLA Ops:
  6.5 1.0 copy-start
  6.5 131.2 %all-gather.3.cloned.1.call-start = ((), (), s32[]{:S(2)}) async-start(), calls=%async_computation.2 | async-start | bytes 4325376 | tf_op jit(solution)/shard_map/all_gather | solution.py:118
  6.8 3.6 %copy-start.19 = (f32[32,32]{0,1:T(8,128)}, f32[32,32]{0,1:T(8,128)S(1)}, u32[]{:S(2)}) copy-start(f32[32,32]{0,1:T(8,128)S(1)} %copy.85) | copy-start | bytes 12292
  7.6 4.6 %copy-start.7 = (f32[32,32]{0,1:T(8,128)}, f32[32,32]{0,1:T(8,128)S(1)}, u32[]{:S(2)}) copy-start(f32[32,32]{0,1:T(8,128)S(1)} %copy.90) | copy-start | bytes 12292
  57.1 1.0 copy-start.3
  59.0 1.9 copy-start.1
  60.8 2.1 %copy-start.2 = (bf16[4,2,256,256]{3,2,1,0:T(8,128)(2,1)S(1)}, bf16[4,2,256,256]{3,2,1,0:T(8,128)(2,1)}, u32[]{:S(2)}) copy-start(bf16[4,2,256,256]{3,2,1,0:T(8,128)(2,1)} %param.7) | copy-start | bytes 3145732
  60.9 2.3 %copy-start.9 = (bf16[2,2,128,128]{2,3,1,0:T(8,128)(2,1)}, bf16[2,2,128,128]{2,3,1,0:T(8,128)(2,1)S(1)}, u32[]{:S(2)}) copy-start(bf16[2,2,128,128]{2,3,1,0:T(8,128)(2,1)S(1)} %multiply_convert_fusion.1) | copy-start | bytes 393220
  60.9 2.6 %copy-start.11 = (bf16[2,2,128,128]{2,3,1,0:T(8,128)(2,1)}, bf16[2,2,128,128]{2,3,1,0:T(8,128)(2,1)S(1)}, u32[]{:S(2)}) copy-start(bf16[2,2,128,128]{2,3,1,0:T(8,128)(2,1)S(1)} %multiply_convert_fusion) | copy-start | bytes 393220
  61.0 2.6 %copy-start.13 = (bf16[2,2,128,128]{2,3,1,0:T(8,128)(2,1)}, bf16[2,2,128,128]{2,3,1,0:T(8,128)(2,1)S(1)}, u32[]{:S(2)}) copy-start(bf16[2,2,128,128]{2,3,1,0:T(8,128)(2,1)S(1)} %broadcast_in_dim.6) | copy-start | bytes 393220
  62.0 2.7 %copy-start.15 = (bf16[2,2,128,128]{2,3,1,0:T(8,128)(2,1)}, bf16[2,2,128,128]{2,3,1,0:T(8,128)(2,1)S(1)}, u32[]{:S(2)}) copy-start(bf16[2,2,128,128]{2,3,1,0:T(8,128)(2,1)S(1)} %broadcast_in_dim.7) | copy-start | bytes 393220
  63.6 74.2 %copy-start.21 = (f32[5]{0:T(128)S(1)}, f32[5]{0:T(128)}, u32[]{:S(2)}) copy-start(f32[5]{0:T(128)} %constant.88.clone) | copy-start | bytes 64
  63.6 74.2 %copy-start.22 = (s32[5]{0:T(128)S(1)}, s32[5]{0:T(128)}, u32[]{:S(2)}) copy-start(s32[5]{0:T(128)} %shift-right-arithmetic_xor_fusion) | copy-start | bytes 64
  144.4 1.1 copy-start.12
  144.4 1.1 copy-start.16
  144.4 1.1 copy-start.18
  144.8 1.0 copy-start.10
  144.8 1.0 copy-start.14
  144.8 1.1 copy-start.17
  145.2 1.1 copy-start.4
  145.6 1.2 copy-start.6
  146.5 1.1 copy-start.5
  153.5 33.1 %copy-start.8 = (f32[32,32]{0,1:T(8,128)S(1)}, f32[32,32]{0,1:T(8,128)}, u32[]{:S(2)}) copy-start(f32[32,32]{0,1:T(8,128)} %copy-done.7) | copy-start | bytes 12292
  153.5 33.0 %all-to-all-start.1 = ((f32[2,32,32,128]{3,2,0,1:T(8,128)}), f32[2,32,32,128]{3,2,0,1:T(8,128)S(1)}, u32[]{:S(2)}, u32[]{:S(2)}) async-start(f32[2,32,32,128]{3,2,0,1:T(8,128)} %copy.129), calls=%async_computation.1 | async-start | bytes 2097152 | tf_op jit(solution)/shard_map/all_to_all | solution.py:153
  187.9 2.6 %copy-start.20 = (f32[32,32]{0,1:T(8,128)S(1)}, f32[32,32]{0,1:T(8,128)}, u32[]{:S(2)}) copy-start(f32[32,32]{0,1:T(8,128)} %copy-done.19) | copy-start | bytes 12292
Sparse Core Ops, SparseCore 0:
  60.3 77.4 all-gather.2
where the time goes:
time: 205 us; the launch traced here: 204 us
  waiting for transfers between devices  97.2 us (47%)
  blocking collectives  39.5 us (19%)
  matrix products  36.3 us (18%)
  between operations  14.1 us (7%)
  starting transfers between devices  7.6 us (4%)
  local copies, waits for them, and re-layouts  7.04 us (3%)
  other arithmetic  2.41 us (1%)
    all_gather x1, waiting for transfers between devices, shards(): every = lax.all_gather(totals[None], 'rows', axis=0, tiled=True)  71.9 us
    all_to_all x1, blocking collectives, shards(): lax.all_to_all(turned, 'rows', split_axis=1, concat_axis=1, tiled=True)  39.5 us
    all_to_all x1, waiting for transfers between devices, shards(): lax.all_to_all(jnp.stack([spectral_re, spectral_im]), 'rows', split_axis=...  25.3 us
    all_to_all x1, starting transfers between devices, shards(): lax.all_to_all(jnp.stack([spectral_re, spectral_im]), 'rows', split_axis=...  7.6 us
    dot_general x1, matrix products, shards(): jnp.einsum('ud,dkrc->ukrc', member, every, precision=lax.Precision.HIGHEST)  5.82 us
    dot_general x5, matrix products, exact_mix(): jnp.einsum(pattern, left_im, right_re, precision=highest)  5.04 us
    dot_general x5, matrix products, exact_mix(): jnp.einsum(pattern, left_im, right_im, precision=highest)  5.01 us
    dot_general x5, matrix products, exact_mix(): jnp.einsum(pattern, left_re, right_im, precision=highest)  4.87 us
  transfers between devices with their start and end apart: 2, of which 2 were waited for; matrix products, arithmetic and copies ran while one was open for 3% of the time, Pallas kernels for 0%

commit v1 on v0

--- a/solution.py
+++ b/solution.py
@@ -115,7 +115,9 @@
         jnp.stack(inner_im),
     )
     totals = jnp.stack([jnp.sum(coeff_re, axis=0), jnp.sum(coeff_im, axis=0)])
-    every = lax.all_gather(totals[None], "rows", axis=0, tiled=True)
+    every = jnp.concatenate(
+        lax.all_to_all(jnp.stack([totals[None]] * lax.axis_size("rows")), "rows", 0, 0), axis=0
+    )
     device_ids = jnp.arange(rows_count, dtype=jnp.int32)
     bit_ids = jnp.arange(up_levels, dtype=jnp.int32)
     partner_group = jnp.bitwise_xor(jnp.right_shift(device, bit_ids), 1)

time: 205 us -> 216 us (1.054)
  waiting for transfers between devices: 97.2 us -> 112 us
  between operations: 14.1 us -> 0.7 us
  starting transfers between devices: 7.6 us -> 14.1 us
  local copies, waits for them, and re-layouts: 7.04 us -> 11.2 us
    all_to_all x0 -> x1, waiting for transfers between devices: none -> 85.3 us  [shards(): lax.all_to_all(jnp.stack([totals[None]] * lax.axis_size('rows')), 'rows',...]
    all_gather x1 -> x0, waiting for transfers between devices: 71.9 us -> none  [shards(): every = lax.all_gather(totals[None], 'rows', axis=0, tiled=True)]
    all_to_all x0 -> x1, starting transfers between devices: none -> 5.63 us  [shards(): lax.all_to_all(jnp.stack([totals[None]] * lax.axis_size('rows')), 'rows',...]
    another operation x0 -> x1, local copies, waits for them, and re-layouts: none -> 2.49 us  [shards(): jnp.stack([totals[None]] * lax.axis_size('rows'))]
  transfers between devices with their start and end apart: 2 -> 2, of which waited for: 2 -> 2; matrix products, arithmetic and copies ran while one was open for 3% -> 2% of each run, Pallas kernels for 0% -> 0%
where the time goes in v1:
time: 216 us
  waiting for transfers between devices  112 us (52%)
  blocking collectives  39.5 us (18%)
  matrix products  37 us (17%)
  starting transfers between devices  14.1 us (7%)
  local copies, waits for them, and re-layouts  11.2 us (5%)
    all_to_all x1, waiting for transfers between devices, shards(): lax.all_to_all(jnp.stack([totals[None]] * lax.axis_size('rows')), 'rows',...  85.3 us
    all_to_all x1, blocking collectives, shards(): lax.all_to_all(turned, 'rows', split_axis=1, concat_axis=1, tiled=True)  39.5 us
    all_to_all x1, waiting for transfers between devices, shards(): lax.all_to_all(jnp.stack([spectral_re, spectral_im]), 'rows', split_axis=...  26.3 us
    all_to_all x1, starting transfers between devices, shards(): lax.all_to_all(jnp.stack([spectral_re, spectral_im]), 'rows', split_axis=...  8.5 us
    dot_general x1, matrix products, shards(): jnp.einsum('ud,dkrc->ukrc', member, every, precision=lax.Precision.HIGHEST)  5.82 us
    all_to_all x1, starting transfers between devices, shards(): lax.all_to_all(jnp.stack([totals[None]] * lax.axis_size('rows')), 'rows',...  5.63 us
    dot_general x5, matrix products, exact_mix(): jnp.einsum(pattern, left_im, right_re, precision=highest)  5.04 us
    dot_general x5, matrix products, exact_mix(): jnp.einsum(pattern, left_im, right_im, precision=highest)  5.02 us
  transfers between devices with their start and end apart: 2, of which 2 were waited for; matrix products, arithmetic and copies ran while one was open for 2% of the time, Pallas kernels for 0%

profile of v1, /device:TPU:2, one launch (start us, length us, event | category | flops | bytes accessed | tf_op | source)
XLA Modules:
  0.0 215.8 jit_solution(11649410760760113087)
XLA Ops:
  0.2 0.9 copy-done
  1.0 0.9 fusion.66
  2.1 1.0 multiply_add_fusion.2
  3.1 0.9 fusion.58
  4.0 0.9 fusion.62
  4.9 0.9 convolution_add_fusion.5
  6.0 1.0 add_bitcast_fusion
  7.2 0.6 copy.93
  7.8 39.5 %all_to_all.15 = f32[2,32,32,128]{3,2,0,1:T(8,128)S(1)} all-to-all(f32[2,32,32,128]{3,2,0,1:T(8,128)S(1)} %copy.93), channel_id=1, replica_groups=mesh['rows'=32,'rhs'=8] {'rows'}, dimensions={1} | all-to-all | bytes 2097152 | tf_op jit(solution)/shard_map/all_to_all | solution.py:90
  47.4 0.9 fusion.44
  48.3 0.9 fusion.45
  49.2 0.9 fusion.16
  50.1 0.9 fusion.15
  51.0 0.1 fusion.29
  51.2 0.1 copy.99
  51.3 0.1 copy.96
  51.4 0.6 copy-done.3
  52.0 0.3 fusion.83
  52.3 0.3 fusion.85
  52.6 0.3 bitcast_reduce_fusion
  52.9 0.3 bitcast_reduce_fusion.1
  53.3 2.5 %stack.60 = f32[32,1,2,128,128]{4,3,2,1,0:T(8,128)} broadcast(f32[2,128,128]{2,1,0:T(8,128)S(1)} %copy.110), dimensions={2,3,4} | broadcast | bytes 4325376 | tf_op jit(solution)/shard_map/stack | solution.py:119
  55.8 5.6 %all-to-all-start.1 = ((f32[32,1,2,128,128]{4,3,2,1,0:T(8,128)}), f32[32,1,2,128,128]{4,3,2,1,0:T(8,128)}, u32[]{:S(2)}, u32[]{:S(2)}) async-start(f32[32,1,2,128,128]{4,3,2,1,0:T(8,128)} %stack.60), calls=%async_computation.1 | async-start | bytes 8388608 | tf_op jit(solution)/shard_map/all_to_all | solution.py:119
  61.7 1.4 copy-done.1
  63.1 0.9 convolution_bitcast_fusion.6
  64.0 0.9 convolution_bitcast_fusion.2
  65.0 0.3 fusion.42
  65.3 0.3 fusion.40
  65.6 1.2 convolution_subtract_fusion.6
  66.8 1.1 convolution_add_fusion.6
  67.9 85.3 %all-to-all-done.1 = f32[32,1,2,128,128]{4,3,2,1,0:T(8,128)} async-done(((f32[32,1,2,128,128]{4,3,2,1,0:T(8,128)}), f32[32,1,2,128,128]{4,3,2,1,0:T(8,128)}, u32[]{:S(2)}, u32[]{:S(2)}) %all-to-all-start.1) | async-done | bytes 4194336 | tf_op jit(solution)/shard_map/all_to_all | solution.py:119
  153.2 5.8 %fusion.6 = bf16[5,2,128,128]{3,0,2,1:T(8,128)(2,1)S(1)} fusion(f32[32,1,2,128,128]{4,3,2,1,0:T(8,128)} %all-to-all-done.1, f32[5]{0:T(128)S(1)} %copy-done.17, s32[5]{0:T(128)S(1)} %shift-right-arithmetic_xor_fusion), kind=kOutput, calls=%fused_computation.4 | convolution fusion | flops 63242560 | bytes 4522024 | tf_op jit(solution)/shard_map/ud,dkrc->ukrc/dot_general | solution.py:127
  159.1 0.2 copy.115
  159.3 0.3 convolution_bitcast_fusion.4
  159.6 0.2 copy.113
  159.9 0.3 convolution_bitcast_fusion
  160.2 0.3 fusion.24
  160.6 0.3 fusion.26
  161.0 0.2 fusion.28
  161.3 0.2 fusion.76
  161.7 0.2 fusion.27
  162.0 0.2 fusion.74
  162.2 0.2 fusion.14
  162.4 0.2 copy.120
  162.6 0.9 fusion.56
  163.6 1.0 fusion.12
  164.6 1.2 copy.124
  165.8 0.9 fusion.52
  166.7 0.9 fusion.10
  167.6 0.9 fusion.9
  168.6 1.6 copy.128
  170.2 8.5 %all-to-all-start.2 = ((f32[2,32,32,128]{3,2,0,1:T(8,128)}), f32[2,32,32,128]{3,2,0,1:T(8,128)S(1)}, u32[]{:S(2)}, u32[]{:S(2)}) async-start(f32[2,32,32,128]{3,2,0,1:T(8,128)} %copy.128), calls=%async_computation.2 | async-start | bytes 2097152 | tf_op jit(solution)/shard_map/all_to_all | solution.py:155
  178.9 26.3 %all-to-all-done.2 = f32[2,32,32,128]{3,2,0,1:T(8,128)S(1)} async-done(((f32[2,32,32,128]{3,2,0,1:T(8,128)}), f32[2,32,32,128]{3,2,0,1:T(8,128)S(1)}, u32[]{:S(2)}, u32[]{:S(2)}) %all-to-all-start.2) | async-done | bytes 1048608 | tf_op jit(solution)/shard_map/all_to_all | solution.py:155
  205.2 1.3 fusion.104
  206.5 1.3 fusion.103
  207.8 1.3 convolution_subtract_fusion.1
  209.1 1.4 multiply_subtract_fusion
  210.6 0.9 fusion.50
  211.5 0.9 fusion.46
  212.3 0.9 convolution_subtract_fusion
  213.2 0.3 copy.134
  213.6 0.9 convolution_add_fusion
  214.5 0.3 copy.137
  214.8 1.1 maximum_multiply_fusion.1
  (59 shorter events, 1.6 us)
Async XLA Ops:
  0.0 1.0 copy-start
  51.0 1.0 copy-start.3
  55.8 97.4 %all-to-all-start.1 = ((f32[32,1,2,128,128]{4,3,2,1,0:T(8,128)}), f32[32,1,2,128,128]{4,3,2,1,0:T(8,128)}, u32[]{:S(2)}, u32[]{:S(2)}) async-start(f32[32,1,2,128,128]{4,3,2,1,0:T(8,128)} %stack.60), calls=%async_computation.1 | async-start | bytes 8388608 | tf_op jit(solution)/shard_map/all_to_all | solution.py:119
  61.4 1.6 copy-start.1
  61.5 3.5 %copy-start.2 = (bf16[4,2,256,256]{3,2,1,0:T(8,128)(2,1)S(1)}, bf16[4,2,256,256]{3,2,1,0:T(8,128)(2,1)}, u32[]{:S(2)}) copy-start(bf16[4,2,256,256]{3,2,1,0:T(8,128)(2,1)} %param.7) | copy-start | bytes 3145732
  61.6 3.7 %copy-start.7 = (bf16[2,2,128,128]{2,3,1,0:T(8,128)(2,1)}, bf16[2,2,128,128]{2,3,1,0:T(8,128)(2,1)S(1)}, u32[]{:S(2)}) copy-start(bf16[2,2,128,128]{2,3,1,0:T(8,128)(2,1)S(1)} %multiply_convert_fusion) | copy-start | bytes 393220
  61.6 4.0 %copy-start.9 = (bf16[2,2,128,128]{2,3,1,0:T(8,128)(2,1)}, bf16[2,2,128,128]{2,3,1,0:T(8,128)(2,1)S(1)}, u32[]{:S(2)}) copy-start(bf16[2,2,128,128]{2,3,1,0:T(8,128)(2,1)S(1)} %multiply_convert_fusion.1) | copy-start | bytes 393220
  61.7 4.0 %copy-start.11 = (bf16[2,2,128,128]{2,3,1,0:T(8,128)(2,1)}, bf16[2,2,128,128]{2,3,1,0:T(8,128)(2,1)S(1)}, u32[]{:S(2)}) copy-start(bf16[2,2,128,128]{2,3,1,0:T(8,128)(2,1)S(1)} %broadcast_in_dim.5) | copy-start | bytes 393220
  64.0 2.8 %copy-start.13 = (bf16[2,2,128,128]{2,3,1,0:T(8,128)(2,1)}, bf16[2,2,128,128]{2,3,1,0:T(8,128)(2,1)S(1)}, u32[]{:S(2)}) copy-start(bf16[2,2,128,128]{2,3,1,0:T(8,128)(2,1)S(1)} %broadcast_in_dim.4) | copy-start | bytes 393220
  65.6 87.6 %copy-start.17 = (f32[5]{0:T(128)S(1)}, f32[5]{0:T(128)}, u32[]{:S(2)}) copy-start(f32[5]{0:T(128)} %constant.88.clone) | copy-start | bytes 64
  159.8 1.1 copy-start.10
  159.9 1.1 copy-start.14
  159.9 1.1 copy-start.16
  160.2 1.1 copy-start.4
  160.6 1.0 copy-start.8
  160.6 1.0 copy-start.12
  160.6 1.1 copy-start.15
  161.0 1.2 copy-start.6
  162.2 1.4 copy-start.5
  170.2 34.9 %all-to-all-start.2 = ((f32[2,32,32,128]{3,2,0,1:T(8,128)}), f32[2,32,32,128]{3,2,0,1:T(8,128)S(1)}, u32[]{:S(2)}, u32[]{:S(2)}) async-start(f32[2,32,32,128]{3,2,0,1:T(8,128)} %copy.128), calls=%async_computation.2 | async-start | bytes 2097152 | tf_op jit(solution)/shard_map/all_to_all | solution.py:155
